TPU v7x, 256 devices: a whole 4x4x8 slice. The times are simulated.
256 devices in a mesh: ctx: 64 (over z, x, core), grp: 4 (over y).
Axes of the slice: x: 4, y: 4, z: 8, core: 2. Of those that a mesh axis runs over, the one named last changes fastest.
Arguments:
- queries: bfloat16 [131072, 512], P('ctx', 'grp'), may hold values from -100 to 100
- kv_cache: bfloat16 [131072, 256], P(('ctx', 'grp')), may hold values from -6 to 6
- grad_out: bfloat16 [131072, 512], P('ctx', 'grp'), may hold values from -6 to 6
- doc_tiles: int32 [32], replicated, may hold values from 1 to 12, 256 in all
Outputs:
- grad_queries: bfloat16 [131072, 512], P('ctx', 'grp')
- grad_kv: bfloat16 [131072, 256], P(('ctx', 'grp'))
All inputs are finite; a program needn't handle non-finite values.
Results may differ from a plain program's by a relative error of at most 0.0059.
Values may be sent and summed in bfloat16 or wider, within the bound.
A program may use at most 64 MiB of HBM per device.

v0:
```python
import math

import jax
import jax.numpy as jnp
from jax import lax
from jax.sharding import PartitionSpec as P

DH = 128
TILE = 512
MAXT = 12


NEG_FILL = -1e30


def passed_along(shard, axis, by):
    devices = lax.axis_size(axis)
    pairs = [(i, i + by) for i in range(devices) if 0 <= i + by < devices]
    return lax.ppermute(shard, axis, pairs)


def document_starts(doc_tiles, tile_count):
    doc_ends = jnp.cumsum(doc_tiles)
    doc_begins = doc_ends - doc_tiles
    tile_ids = jnp.arange(tile_count, dtype=jnp.int32)
    inside = (tile_ids[:, None] >= doc_begins[None, :]) & (tile_ids[:, None] < doc_ends[None, :])
    return jnp.sum(jnp.where(inside, doc_begins[None, :], 0), axis=1)


def shards(queries, kv_cache, grad_out, doc_tiles):
    head_dim = DH
    tile_len = TILE
    local_tokens = queries.shape[0]
    local_tiles = local_tokens // tile_len
    reach = (MAXT - 2) // local_tiles + 1
    heads = queries.shape[1] // head_dim
    scale = 1.0 / math.sqrt(head_dim)
    ctx_count = lax.axis_size("ctx")
    ctx_index = lax.axis_index("ctx")
    group_block = lax.all_gather(kv_cache, "grp", axis=0, tiled=True)
    blocks = []
    for distance in range(reach, 0, -1):
        blocks.append(passed_along(group_block, "ctx", distance))
    blocks.append(group_block)
    window = jnp.stack(blocks)
    window = window.reshape((reach + 1) * local_tiles, tile_len, 2 * head_dim)
    tile_count = ctx_count * local_tiles
    starts = document_starts(doc_tiles, tile_count)
    all_tile_ids = jnp.arange(tile_count, dtype=jnp.int32)
    window_base = (ctx_index - reach) * local_tiles
    query_tiles = queries.reshape(local_tiles, tile_len, heads, head_dim)
    grad_tiles = grad_out.reshape(local_tiles, tile_len, heads, head_dim)
    row_ids = jnp.arange(tile_len, dtype=jnp.int32)
    causal = row_ids[:, None] >= row_ids[None, :]

    def per_tile(window_grad, inputs):
        q_tile, g_tile, local_pos = inputs
        tile_pos = ctx_index * local_tiles + local_pos
        first_tile = jnp.sum(jnp.where(all_tile_ids == tile_pos, starts, 0))

        def scores_at(key_pos):
            kv_tile = lax.dynamic_index_in_dim(window, key_pos - window_base, 0, keepdims=False)
            raw = (
                jnp.einsum(
                    "qhd,kd->hqk", q_tile, kv_tile[:, :head_dim], preferred_element_type=jnp.float32
                )
                * scale
            )
            keep = jnp.logical_or(key_pos != tile_pos, causal)
            return (jnp.where(keep[None], raw, NEG_FILL), kv_tile)

        def first_pass(key_pos, carry):
            row_top, row_total = carry
            scores, _ = scores_at(key_pos)
            new_top = jnp.maximum(row_top, jnp.max(scores, axis=2))
            row_total = row_total * jnp.exp(row_top - new_top) + jnp.sum(
                jnp.exp(scores - new_top[..., None]), axis=2
            )
            return (new_top, row_total)

        start_carry = (
            jnp.full((heads, tile_len), NEG_FILL, jnp.float32),
            jnp.zeros((heads, tile_len), jnp.float32),
        )
        row_top, row_total = lax.fori_loop(first_tile, tile_pos + 1, first_pass, start_carry)
        log_norm = row_top + jnp.log(row_total)

        def second_pass(key_pos, attended):
            scores, kv_tile = scores_at(key_pos)
            probs_low = jnp.exp(scores - log_norm[..., None]).astype(jnp.bfloat16)
            return attended + jnp.einsum(
                "hqk,kd->hqd", probs_low, kv_tile[:, head_dim:], preferred_element_type=jnp.float32
            )

        attended = lax.fori_loop(
            first_tile,
            tile_pos + 1,
            second_pass,
            jnp.zeros((heads, tile_len, head_dim), jnp.float32),
        )
        delta = jnp.einsum("qhd,hqd->hq", g_tile.astype(jnp.float32), attended)

        def third_pass(key_pos, carry):
            grad_q, grad_window = carry
            scores, kv_tile = scores_at(key_pos)
            probs = jnp.exp(scores - log_norm[..., None])
            probs_low = probs.astype(jnp.bfloat16)
            dprobs = jnp.einsum(
                "qhd,kd->hqk", g_tile, kv_tile[:, head_dim:], preferred_element_type=jnp.float32
            )
            dscore = (probs * (dprobs - delta[..., None])).astype(jnp.bfloat16)
            grad_q = grad_q + jnp.einsum(
                "hqk,kd->qhd", dscore, kv_tile[:, :head_dim], preferred_element_type=jnp.float32
            )
            grad_key = jnp.einsum("hqk,qhd->kd", dscore, q_tile, preferred_element_type=jnp.float32)
            grad_value = jnp.einsum(
                "hqk,qhd->kd", probs_low, g_tile, preferred_element_type=jnp.float32
            )
            slot_pos = key_pos - window_base
            previous = lax.dynamic_index_in_dim(grad_window, slot_pos, 0, keepdims=False)
            updated = previous + jnp.concatenate([grad_key, grad_value], axis=1)
            grad_window = lax.dynamic_update_index_in_dim(grad_window, updated, slot_pos, 0)
            return (grad_q, grad_window)

        start_grad = (jnp.zeros((tile_len, heads, head_dim), jnp.float32), window_grad)
        grad_q, window_grad = lax.fori_loop(first_tile, tile_pos + 1, third_pass, start_grad)
        grad_q_low = (grad_q * scale).astype(jnp.bfloat16).reshape(tile_len, heads * head_dim)
        return (window_grad, grad_q_low)

    window_grad = jnp.zeros(((reach + 1) * local_tiles, tile_len, 2 * head_dim), jnp.float32)
    local_positions = jnp.arange(local_tiles, dtype=jnp.int32)
    window_grad, grad_q_all = lax.scan(
        per_tile, window_grad, (query_tiles, grad_tiles, local_positions)
    )
    grad_queries = grad_q_all.reshape(local_tokens, heads * head_dim)
    window_grad = window_grad.reshape(reach + 1, local_tokens, 2 * head_dim)
    own_block = window_grad[reach]
    for distance in range(1, reach + 1):
        own_block = own_block + passed_along(window_grad[reach - distance], "ctx", -distance)
    owned = lax.psum_scatter(own_block, "grp", scatter_dimension=0, tiled=True)
    grad_kv = jnp.concatenate([owned[:, :head_dim] * scale, owned[:, head_dim:]], axis=1).astype(
        jnp.bfloat16
    )
    return (grad_queries, grad_kv)


def solution(mesh):
    placed = (P("ctx", "grp"), P(("ctx", "grp"), None), P("ctx", "grp"), P())
    return jax.shard_map(
        shards,
        mesh=mesh,
        in_specs=placed,
        out_specs=(P("ctx", "grp"), P(("ctx", "grp"), None)),
        check_vma=False,
    )
```

profile of v0, /device:TPU:16, one launch (start us, length us, event | category | flops | bytes accessed | tf_op | source)
XLA Modules:
  0.0 678.4 jit_solution(16104952040991135013)
XLA Ops:
  7.9 30.3 %all-gather.2.cloned.1.call-done = bf16[2048,256]{1,0:T(8,128)(2,1)} async-done(((bf16[512,256]{1,0:T(8,128)(2,1)}), bf16[2048,256]{1,0:T(8,128)(2,1)}) %all-gather.2.cloned.1.call-update) | async-done | bytes 1048592 | tf_op jit(solution)/shard_map/all_gather | solution.py:40
  38.2 1.3 collective-permute-start.2
  39.6 4.0 collective-permute-start.1
  43.6 4.0 collective-permute-start
  49.3 18.2 %collective-permute-done.1 = bf16[2048,256]{1,0:T(8,128)(2,1)S(1)} collective-permute-done((bf16[2048,256]{1,0:T(8,128)(2,1)}, bf16[2048,256]{1,0:T(8,128)(2,1)S(1)}, u32[]{:S(2)}, u32[]{:S(2)}) %collective-permute-start.1) | collective-permute-done | bytes 1048608 | tf_op jit(solution)/shard_map/ppermute | solution.py:19
  67.4 22.5 %collective-permute-done = bf16[2048,256]{1,0:T(8,128)(2,1)S(1)} collective-permute-done((bf16[2048,256]{1,0:T(8,128)(2,1)}, bf16[2048,256]{1,0:T(8,128)(2,1)S(1)}, u32[]{:S(2)}, u32[]{:S(2)}) %collective-permute-start) | collective-permute-done | bytes 1048608 | tf_op jit(solution)/shard_map/ppermute | solution.py:19
  89.9 3.3 pad_maximum_fusion
  93.2 4.3 broadcast_in_dim.54
  97.5 121.0 %while.80 = (s32[]{:T(128)}, f32[16,512,256]{1,2,0:T(8,128)}, bf16[4,512,128]{2,1,0:T(8,128)(2,1)}, s32[4]{0:T(128)S(1)}, s32[]{:T(128)}, /*index=5*/s32[256]{0:...) while((s32[]{:T(128)}, f32[16,512,256]{1,2,0:T(8,128)}, ...), condition=%wide.region_12.13_spmd.clone.clone, body=%wide.region_2.12_spmd.clone.clone.sunk | while | flops 542836480 | bytes 16562340 | solution.py:132
  101.8 1.6 while.81
  103.5 1.7 while.82
  105.4 7.0 %while.83 = (s32[]{:T(128)}, f32[512,1,128]{0,2,1:T(8,128)S(1)}, f32[16,512,256]{1,2,0:T(8,128)}, s32[]{:T(128)}, s32[]{:T(128)}, /*index=5*/bf16[16,512,256]{2,...) while((s32[]{:T(128)}, f32[512,1,128]{0,2,1:T(8,128)S(1)}, ...), condition=%wide.region_11.11_spmd, body=%wide.region_10.10_spmd.sunk | while | flops 337969152 | bytes 9048277 | solution.py:126
  109.3 1.9 fusion.100
  117.5 3.2 while.81
  120.8 3.4 while.82
  124.4 13.4 %while.83 = (s32[]{:T(128)}, f32[512,1,128]{0,2,1:T(8,128)S(1)}, f32[16,512,256]{1,2,0:T(8,128)}, s32[]{:T(128)}, s32[]{:T(128)}, /*index=5*/bf16[16,512,256]{2,...) while((s32[]{:T(128)}, f32[512,1,128]{0,2,1:T(8,128)S(1)}, ...), condition=%wide.region_11.11_spmd, body=%wide.region_10.10_spmd.sunk | while | flops 337969152 | bytes 9048277 | solution.py:126
  125.7 1.0 dynamic-slice_bitcast_fusion.12
  128.3 1.9 fusion.100
  132.1 1.0 dynamic-slice_bitcast_fusion.12
  134.7 1.9 fusion.100
  142.9 4.8 while.81
  147.8 5.1 while.82
  153.1 19.7 %while.83 = (s32[]{:T(128)}, f32[512,1,128]{0,2,1:T(8,128)S(1)}, f32[16,512,256]{1,2,0:T(8,128)}, s32[]{:T(128)}, s32[]{:T(128)}, /*index=5*/bf16[16,512,256]{2,...) while((s32[]{:T(128)}, f32[512,1,128]{0,2,1:T(8,128)S(1)}, ...), condition=%wide.region_11.11_spmd, body=%wide.region_10.10_spmd.sunk | while | flops 337969152 | bytes 9048277 | solution.py:126
  157.0 1.9 fusion.100
  163.4 1.9 fusion.100
  169.8 1.9 fusion.100
  178.0 6.4 while.81
  184.5 6.9 %while.82 = (s32[]{:T(128)}, f32[1,512,128]{2,1,0:T(8,128)S(1)}, s32[]{:T(128)}, s32[]{:T(128)}, pred[512,512]{0,1:T(32,128)(4,1)S(1)}, /*index=5*/s32[]{:T(128)...) while((s32[]{:T(128)}, f32[1,512,128]{2,1,0:T(8,128)S(1)}, ...), condition=%wide.region_9.9_spmd, body=%wide.region_8.8_spmd.sunk | while | flops 135593984 | bytes 1706169 | solution.py:95
  184.5 1.0 dynamic-slice_bitcast_fusion.11
  186.2 1.0 dynamic-slice_bitcast_fusion.11
  191.5 26.1 %while.83 = (s32[]{:T(128)}, f32[512,1,128]{0,2,1:T(8,128)S(1)}, f32[16,512,256]{1,2,0:T(8,128)}, s32[]{:T(128)}, s32[]{:T(128)}, /*index=5*/bf16[16,512,256]{2,...) while((s32[]{:T(128)}, f32[512,1,128]{0,2,1:T(8,128)S(1)}, ...), condition=%wide.region_11.11_spmd, body=%wide.region_10.10_spmd.sunk | while | flops 337969152 | bytes 9048277 | solution.py:126
  195.4 1.9 fusion.100
  201.8 1.9 fusion.100
  208.2 1.9 fusion.100
  214.5 1.9 fusion.100
  218.5 6.5 fusion.54
  225.0 2.9 copy.21
  227.9 2.9 copy.23
  230.8 1.8 copy.22
  232.7 1.3 collective-permute-start.4
  234.0 1.3 collective-permute-start.5
  235.3 1.3 collective-permute-start.3
  236.6 1.9 copy.20
  238.5 70.1 %collective-permute-done.4 = f32[2048,256]{1,0:T(8,128)} collective-permute-done((f32[2048,256]{1,0:T(8,128)}, f32[2048,256]{1,0:T(8,128)}, u32[]{:S(2)}, u32[]{:S(2)}) %collective-permute-start.4) | collective-permute-done | bytes 2097184 | tf_op jit(solution)/shard_map/ppermute | solution.py:19
  308.6 159.9 %collective-permute-done.5 = f32[2048,256]{1,0:T(8,128)} collective-permute-done((f32[2048,256]{1,0:T(8,128)}, f32[2048,256]{1,0:T(8,128)}, u32[]{:S(2)}, u32[]{:S(2)}) %collective-permute-start.5) | collective-permute-done | bytes 2097184 | tf_op jit(solution)/shard_map/ppermute | solution.py:19
  468.5 4.7 fusion.50
  473.2 195.7 %reduce-scatter.2.cloned.1.call-done = f32[512,256]{1,0:T(8,128)} async-done(((f32[2048,256]{1,0:T(8,128)}), f32[512,256]{1,0:T(8,128)}) %reduce-scatter.2.cloned.1.call-update) | async-done | bytes 524304 | tf_op jit(solution)/shard_map/reduce_scatter | solution.py:140
  669.8 1.0 fusion.51
  (205 shorter events, 71.5 us)
Async XLA Ops:
  7.2 31.1 %all-gather.2.cloned.1.call-start = ((), (), s32[]{:S(2)}) async-start(), calls=%async_computation.1 | async-start | bytes 1310720 | tf_op jit(solution)/shard_map/all_gather | solution.py:40
  7.9 661.0 %reduce-scatter.2.cloned.1.call-start = ((), (), s32[]{:S(2)}) async-start(), calls=%async_computation.2 | async-start | bytes 2621440 | tf_op jit(solution)/shard_map/reduce_scatter | solution.py:140
  38.2 11.0 %collective-permute-start.2 = (bf16[2048,256]{1,0:T(8,128)(2,1)}, bf16[2048,256]{1,0:T(8,128)(2,1)S(1)}, u32[]{:S(2)}, u32[]{:S(2)}) collective-permute-start(bf16[2048,256]{1,0:T(8,128)(2,1)} %all-gather.2.cloned.1.call-done), channel_id=1, source_target_pairs={{0,4},{4,8},{8,12},{12,16},{16,20},{20,24},{24,28},{28,32},{32,36}... | collective-permute-start | bytes 3145736 | tf_op jit(solution)/shard_map/ppermute | solution.py:19
  39.6 27.9 %collective-permute-start.1 = (bf16[2048,256]{1,0:T(8,128)(2,1)}, bf16[2048,256]{1,0:T(8,128)(2,1)S(1)}, u32[]{:S(2)}, u32[]{:S(2)}) collective-permute-start(bf16[2048,256]{1,0:T(8,128)(2,1)} %all-gather.2.cloned.1.call-done), channel_id=1, source_target_pairs={{0,8},{4,12},{8,16},{12,20},{16,24},{20,28},{24,32},{28,36},{32,40... | collective-permute-start | bytes 3145736 | tf_op jit(solution)/shard_map/ppermute | solution.py:19
  43.6 46.3 %collective-permute-start = (bf16[2048,256]{1,0:T(8,128)(2,1)}, bf16[2048,256]{1,0:T(8,128)(2,1)S(1)}, u32[]{:S(2)}, u32[]{:S(2)}) collective-permute-start(bf16[2048,256]{1,0:T(8,128)(2,1)} %all-gather.2.cloned.1.call-done), channel_id=1, source_target_pairs={{0,12},{4,16},{8,20},{12,24},{16,28},{20,32},{24,36},{28,40},{32,4... | collective-permute-start | bytes 3145736 | tf_op jit(solution)/shard_map/ppermute | solution.py:19
  93.2 4.3 copy-start
  232.7 75.9 %collective-permute-start.4 = (f32[2048,256]{1,0:T(8,128)}, f32[2048,256]{1,0:T(8,128)}, u32[]{:S(2)}, u32[]{:S(2)}) collective-permute-start(f32[2048,256]{1,0:T(8,128)} %bitcast.227), channel_id=1, source_target_pairs={{8,0},{12,4},{16,8},{20,12},{24,16},{28,20},{32,24},{36,28},{40,32... | collective-permute-start | bytes 6291464 | tf_op jit(solution)/shard_map/ppermute | solution.py:19
  234.0 234.5 %collective-permute-start.5 = (f32[2048,256]{1,0:T(8,128)}, f32[2048,256]{1,0:T(8,128)}, u32[]{:S(2)}, u32[]{:S(2)}) collective-permute-start(f32[2048,256]{1,0:T(8,128)} %bitcast.226), channel_id=1, source_target_pairs={{12,0},{16,4},{20,8},{24,12},{28,16},{32,20},{36,24},{40,28},{44,3... | collective-permute-start | bytes 6291464 | tf_op jit(solution)/shard_map/ppermute | solution.py:19
  235.3 233.2 %collective-permute-start.3 = (f32[2048,256]{1,0:T(8,128)}, f32[2048,256]{1,0:T(8,128)}, u32[]{:S(2)}, u32[]{:S(2)}) collective-permute-start(f32[2048,256]{1,0:T(8,128)} %bitcast.225), channel_id=1, source_target_pairs={{4,0},{8,4},{12,8},{16,12},{20,16},{24,20},{28,24},{32,28},{36,32}... | collective-permute-start | bytes 6291464 | tf_op jit(solution)/shard_map/ppermute | solution.py:19
Sparse Core Ops, SparseCore 0:
  9.8 28.3 all-gather.1
  473.3 195.5 reduce-scatter.1
where the time goes:
time: 688 us; the launch traced here: 678 us
  waiting for transfers between devices  497 us (72%)
  local copies, waits for them, and re-layouts  61 us (9%)
  other arithmetic  35.9 us (5%)
  loops' own time  30.4 us (4%)
  matrix products  26.5 us (4%)
  between operations  14.1 us (2%)
  starting transfers between devices  13.3 us (2%)
    ppermute x6, waiting for transfers between devices, passed_along(): return lax.ppermute(shard, axis, pairs)  271 us
    reduce_scatter x1, waiting for transfers between devices, shards(): owned = lax.psum_scatter(own_block, 'grp', scatter_dimension=0, tiled=True)  196 us
    all_gather x1, waiting for transfers between devices, shards(): group_block = lax.all_gather(kv_cache, 'grp', axis=0, tiled=True)  30.3 us
    squeeze x30, local copies, waits for them, and re-layouts, scores_at(): lax.dynamic_index_in_dim(window, key_pos - window_base, 0, keepdims=False)  29.2 us
    another operation x4, loops' own time, per_tile(): lax.fori_loop(first_tile, tile_pos + 1, third_pass, start_grad)  21.2 us
    dynamic_update_slice x10, other arithmetic, third_pass(): lax.dynamic_update_index_in_dim(grad_window, updated, slot_pos, 0)  19.3 us
  transfers between devices with their start and end apart: 8, of which 6 were waited for; matrix products, arithmetic and copies ran while one was open for 1% of the time, Pallas kernels for 0%

commit v1 on v0

v1 whole, which is shorter than its diff:
```python
import functools
import math

import jax
import jax.numpy as jnp
from jax import lax
from jax.experimental import pallas as pl
from jax.experimental.pallas import tpu as pltpu
from jax.sharding import PartitionSpec as P

DH = 128
TILE = 512
HALF = TILE // 2
LOCAL = 4
WINDOW = 16
SCALE = 1.0 / math.sqrt(DH)
C = SCALE * math.log2(math.e)
LOW = -1e30
f32 = jnp.float32
bf16 = jnp.bfloat16
MESH = pl.DeviceIdType.MESH


def dot(a, b, dims):
    return lax.dot_general(a, b, (dims, ((), ())), preferred_element_type=f32)


NT = ((1,), (1,))
NN = ((1,), (0,))


def document_starts(doc_tiles, tile_count):
    doc_ends = jnp.cumsum(doc_tiles)
    doc_begins = doc_ends - doc_tiles
    tile_ids = jnp.arange(tile_count, dtype=jnp.int32)
    inside = (tile_ids[:, None] >= doc_begins[None, :]) & (tile_ids[:, None] < doc_ends[None, :])
    return jnp.sum(jnp.where(inside, doc_begins[None, :], 0), axis=1)


def kernel(
    ctx_count,
    first_ref, q_ref, g_ref, kv_ref,
    dq_ref, dkv_ref,
    kvw, stage, ddA, ddB, half, full, xin, acc, own, dqt, m_s, l_s, d_s,
    sendG, sendD, sendX, recvA, recvB,
    bsendD, brecvA, brecvB, bsendG, brecvG, bsendX, brecvX,
):
    c = lax.axis_index("ctx")
    y = lax.axis_index("grp")
    k = lax.rem(c, 2)
    other = c + 1 - 2 * k
    yR, yO, yL = (y + 1) % 4, (y + 2) % 4, (y + 3) % 4
    up = lambda n: (c + n) % ctx_count
    down = lambda n: (c + ctx_count - n) % ctx_count

    def remote(src, dst, ssem, rsem, dev):
        return pltpu.make_async_remote_copy(
            src_ref=src, dst_ref=dst, send_sem=ssem, recv_sem=rsem, device_id=dev, device_id_type=MESH
        )

    def landed(ref, sem):
        remote(ref, ref, sem, sem, (other, y)).wait_recv()

    def gone(ref, sem):
        remote(ref, ref, sem, sem, (other, y)).wait_send()

    kvw[12 + y] = kv_ref[...]
    m_s[...] = jnp.full_like(m_s, LOW)
    l_s[...] = jnp.zeros_like(l_s)
    d_s[...] = jnp.zeros_like(d_s)

    barrier = pltpu.get_barrier_semaphore()
    far = (c + ctx_count + 6 * k - 3) % ctx_count
    for dev in ((other, y), (c, yR), (c, yL), (up(2), y), (down(2), y), (far, y)):
        pl.semaphore_signal(barrier, inc=1, device_id=dev, device_id_type=MESH)
    pl.semaphore_wait(barrier, 6)

    def share(group, base):
        src = kvw.at[base + y]
        remote(src, src, sendG.at[group, 0], recvA.at[base + y], (c, yR)).start()
        remote(src, src, sendG.at[group, 1], recvA.at[base + y], (c, yL)).start()

    def relay(group, base):
        landed(kvw.at[base + yL], recvA.at[base + yL])
        top = kvw.at[base + yL, pl.ds(0, HALF)]
        remote(top, top, sendG.at[group, 2], recvA.at[base + yL], (c, yR)).start()
        landed(kvw.at[base + yR], recvA.at[base + yR])
        low = kvw.at[base + yR, pl.ds(HALF, HALF)]
        remote(low, low, sendG.at[group, 3], recvB.at[base + yR], (c, yL)).start()

    def last_in(base):
        landed(kvw.at[base + yO, pl.ds(0, HALF)], recvA.at[base + yO])
        landed(kvw.at[base + yO, pl.ds(HALF, HALF)], recvB.at[base + yO])

    def across(src, dst):
        remote(kvw.at[src], kvw.at[dst], sendD.at[src], recvA.at[dst], (other, y)).start()

    def across_own(u):
        @pl.when(k == 0)
        def _():
            across(12 + u, 8 + u)

    def across_second(u):
        across(4 + u, 8 * k + u)

    share(0, 12)
    mine = kvw.at[12 + y]
    remote(mine, kvw.at[4 + y], sendX.at[0], recvA.at[4 + y], (up(2), y)).start()

    @pl.when(k == 1)
    def _():
        remote(mine, kvw.at[y], sendX.at[1], recvA.at[y], (up(3), y)).start()

    across_own(y)

    causal = lax.broadcasted_iota(jnp.int32, (TILE, TILE), 1) >= lax.broadcasted_iota(
        jnp.int32, (TILE, TILE), 0
    )

    def forward_pair(slot, keys, values, t, diagonal):
        scores = dot(keys, q_ref[t], NT) * C
        if diagonal:
            scores = jnp.where(causal, scores, LOW)
        m = m_s[t]
        valid = first_ref[t] <= slot
        new_m = jnp.where(valid, jnp.maximum(m, jnp.max(scores, axis=0, keepdims=True)), m)
        e = jnp.exp2(scores - jnp.where(valid, new_m, -LOW))
        dp = dot(values, g_ref[t], NT)
        fade = jnp.exp2(m - new_m)
        m_s[t] = new_m
        l_s[t] = l_s[t] * fade + jnp.sum(e, axis=0, keepdims=True)
        d_s[t] = d_s[t] * fade + jnp.sum(e * dp, axis=0, keepdims=True)

    def split(slot):
        tile = kvw[slot]
        return tile[:, :DH], tile[:, DH:]

    def in_order(r):
        return (y + 3 * r - 5 * (r // 2) - 2 * (r // 3) + 4) % 4

    def forward_own(r, carry):
        @pl.when(r == 1)
        def _():
            relay(0, 12)
            across_own(yL)
            across_own(yR)

        @pl.when(r == 2)
        def _():
            landed(kvw.at[4 + y], recvA.at[4 + y])
            share(1, 4)
            across_second(y)

        @pl.when(r == 3)
        def _():
            last_in(12)
            across_own(yO)

            @pl.when(k == 0)
            def _():
                landed(kvw.at[y], recvA.at[y])
                share(2, 0)

        u = in_order(r)
        slot = 12 + u
        forward_pair(slot, *split(slot), u, True)

        def below(t, carry):
            forward_pair(slot, *split(slot), t, False)
            return carry

        return lax.fori_loop(u + 1, LOCAL, below, carry)

    lax.fori_loop(0, 4, forward_own, 0)

    def forward_full(i, carry):
        r = i % 4
        u = in_order(r)
        base = 4 + 4 * ((i // 4 + k) % 2)

        @pl.when(i == 1)
        def _():
            relay(1, 4)
            across_second(yL)
            across_second(yR)

        @pl.when(i == 3)
        def _():
            last_in(4)
            across_second(yO)

        @pl.when(jnp.logical_and(i == 4, k == 0))
        def _():
            relay(2, 0)

        @pl.when(jnp.logical_and(i == 6, k == 0))
        def _():
            last_in(0)

        @pl.when(base == 8)
        def _():
            landed(kvw.at[8 + u], recvA.at[8 + u])

        slot = base + u
        keys, values = split(slot)
        for t in range(LOCAL):
            forward_pair(slot, keys, values, t, False)
        return carry

    lax.fori_loop(0, 8, forward_full, 0)

    def forward_far(r, carry):
        u = in_order(r)

        @pl.when(k == 1)
        def _():
            landed(kvw.at[u], recvA.at[u])

        def above(t, carry):
            forward_pair(u, *split(u), t, False)
            return carry

        return lax.fori_loop(0, u, above, carry)

    lax.fori_loop(0, 4, forward_far, 0)

    for t in range(LOCAL):
        total = l_s[t]
        m_s[t] = m_s[t] + jnp.log2(total)
        d_s[t] = d_s[t] / total
    dqt[...] = jnp.zeros_like(dqt)

    def settle(group, base):
        gone(kvw.at[base + y], sendG.at[group, 0])
        gone(kvw.at[base + y], sendG.at[group, 1])
        gone(kvw.at[base + yL, pl.ds(0, HALF)], sendG.at[group, 2])
        gone(kvw.at[base + yR, pl.ds(HALF, HALF)], sendG.at[group, 3])

    settle(0, 12)
    settle(1, 4)
    gone(mine, sendX.at[0])
    for u in range(4):
        gone(kvw.at[4 + u], sendD.at[4 + u])

    @pl.when(k == 0)
    def _():
        settle(2, 0)
        for u in range(4):
            gone(kvw.at[12 + u], sendD.at[12 + u])

    @pl.when(k == 1)
    def _():
        gone(mine, sendX.at[1])

    def backward_pair(slot, keys, values, keys_t, t, diagonal):
        q, g = q_ref[t], g_ref[t]
        x = dot(keys, q, NT) * C - jnp.where(first_ref[t] <= slot, m_s[t], -LOW)
        if diagonal:
            x = jnp.where(causal, x, LOW)
        p = jnp.exp2(x)
        ds = (p * (dot(values, g, NT) - d_s[t])).astype(bf16)
        dqt[t] += dot(keys_t, ds, NN)
        return dot(ds, q, NN), dot(p.astype(bf16), g, NN)

    def to_y(r):
        return (y + 2 - r + 3 * (r // 2) - 2 * (r // 3) + 4) % 4

    def clear():
        acc[...] = jnp.zeros_like(acc)

    def one_pair(slot, t, diagonal):
        keys, values = split(slot)
        dk, dv = backward_pair(slot, keys, values, keys.astype(f32).T.astype(bf16), t, diagonal)
        acc[:, :DH] += dk
        acc[:, DH:] += dv

    def reduce_step(group, r, u, keep):
        part = stage.at[group, u]

        @pl.when(r == 0)
        def _():
            part[...] = acc[...].astype(bf16)
            remote(
                part.at[pl.ds(0, HALF)], half.at[group, 0],
                bsendG.at[group, 0], brecvG.at[group, 0], (c, yR),
            ).start()
            remote(
                part.at[pl.ds(HALF, HALF)], half.at[group, 1],
                bsendG.at[group, 1], brecvG.at[group, 1], (c, yL),
            ).start()

        @pl.when(r == 1)
        def _():
            landed(half.at[group, 0], brecvG.at[group, 0])
            acc[:HALF] += half[group, 0].astype(f32)
            part[...] = acc[...].astype(bf16)
            remote(part, full.at[group, 0], bsendG.at[group, 2], brecvG.at[group, 2], (c, yR)).start()

        @pl.when(r == 2)
        def _():
            landed(half.at[group, 1], brecvG.at[group, 1])
            acc[HALF:] += half[group, 1].astype(f32)
            part[...] = acc[...].astype(bf16)
            remote(part, full.at[group, 1], bsendG.at[group, 3], brecvG.at[group, 3], (c, yL)).start()

        @pl.when(r == 3)
        def _():
            keep[...] = acc[...]

    def reduced(group, keep):
        landed(full.at[group, 0], brecvG.at[group, 2])
        landed(full.at[group, 1], brecvG.at[group, 3])
        return keep[...] + full[group, 0].astype(f32) + full[group, 1].astype(f32)

    def reduce_gone(group):
        gone(stage.at[group, yO, pl.ds(0, HALF)], bsendG.at[group, 0])
        gone(stage.at[group, yO, pl.ds(HALF, HALF)], bsendG.at[group, 1])
        gone(stage.at[group, yR], bsendG.at[group, 2])
        gone(stage.at[group, yL], bsendG.at[group, 3])

    def backward_far(r, carry):
        u = to_y(r)
        clear()

        def above(t, carry):
            one_pair(u, t, False)
            return carry

        lax.fori_loop(0, u, above, 0)

        @pl.when(k == 0)
        def _():
            reduce_step(2, r, u, own.at[1])

        @pl.when(k == 1)
        def _():
            stage[2, u] = acc[...].astype(bf16)
            remote(stage.at[2, u], ddA.at[u], bsendD.at[0, u], brecvA.at[u], (other, y)).start()

        return carry

    lax.fori_loop(0, 4, backward_far, 0)

    def backward_full(i, carry):
        r = i % 4
        u = to_y(r)
        base = 8 - 4 * (i // 4)
        slot = base + u
        keys, values = split(slot)
        keys_t = keys.T
        dk, dv = backward_pair(slot, keys, values, keys_t, 0, False)
        for t in range(1, LOCAL):
            dk_t, dv_t = backward_pair(slot, keys, values, keys_t, t, False)
            dk += dk_t
            dv += dv_t
        acc[:, :DH] = dk
        acc[:, DH:] = dv

        @pl.when(i < 4)
        def _():
            stage[3, u] = acc[...].astype(bf16)
            remote(stage.at[3, u], ddB.at[u], bsendD.at[1, u], brecvB.at[u], (other, y)).start()

            @pl.when(jnp.logical_and(i == 2, k == 0))
            def _():
                stage[2, y] = reduced(2, own.at[1]).astype(bf16)
                remote(stage.at[2, y], xin.at[1], bsendX.at[1], brecvX.at[1], (down(3), y)).start()

        @pl.when(i >= 4)
        def _():
            @pl.when(k == 0)
            def _():
                landed(ddA.at[u], brecvA.at[u])
                acc[...] += ddA[u].astype(f32)

            @pl.when(k == 1)
            def _():
                landed(ddB.at[u], brecvB.at[u])
                acc[...] += ddB[u].astype(f32)

            reduce_step(1, r, u, own.at[1])

        return carry

    lax.fori_loop(0, 8, backward_full, 0)

    def backward_own(r, carry):
        u = to_y(r)
        slot = 12 + u
        clear()
        one_pair(slot, u, True)

        def below(t, carry):
            one_pair(slot, t, False)
            return carry

        lax.fori_loop(u + 1, LOCAL, below, 0)

        @pl.when(k == 0)
        def _():
            landed(ddB.at[u], brecvB.at[u])
            acc[...] += ddB[u].astype(f32)

        @pl.when(r == 1)
        def _():
            stage[1, y] = reduced(1, own.at[1]).astype(bf16)
            remote(stage.at[1, y], xin.at[0], bsendX.at[0], brecvX.at[0], (down(2), y)).start()

        reduce_step(0, r, u, own.at[0])
        return carry

    lax.fori_loop(0, 4, backward_own, 0)

    for t in range(LOCAL):
        dq_ref[t] = (dqt[t].T * SCALE).astype(bf16)

    landed(xin.at[0], brecvX.at[0])
    own[0] = own[0] + xin[0].astype(f32)

    @pl.when(k == 1)
    def _():
        landed(xin.at[1], brecvX.at[1])
        own[0] = own[0] + xin[1].astype(f32)

    total = reduced(0, own.at[0])
    dkv_ref[:, :DH] = (total[:, :DH] * SCALE).astype(bf16)
    dkv_ref[:, DH:] = total[:, DH:].astype(bf16)

    reduce_gone(0)
    reduce_gone(1)
    gone(stage.at[1, y], bsendX.at[0])
    for u in range(4):
        gone(stage.at[3, u], bsendD.at[1, u])

    @pl.when(k == 0)
    def _():
        reduce_gone(2)
        gone(stage.at[2, y], bsendX.at[1])

    @pl.when(k == 1)
    def _():
        for u in range(4):
            gone(stage.at[2, u], bsendD.at[0, u])


def shards(queries, kv_cache, grad_out, doc_tiles):
    ctx_count = lax.axis_size("ctx")
    c = lax.axis_index("ctx")
    tile_count = ctx_count * LOCAL
    starts = document_starts(doc_tiles, tile_count)
    firsts = lax.dynamic_slice(starts, (c * LOCAL,), (LOCAL,)) - (c * LOCAL - 12)
    firsts = jnp.broadcast_to(firsts[:, None, None], (LOCAL, 1, TILE)).astype(jnp.int32)
    vmem = pl.BlockSpec(memory_space=pltpu.VMEM)
    tile = (TILE, 2 * DH)
    halved = (HALF, 2 * DH)
    row = pltpu.VMEM((LOCAL, 1, TILE), f32)
    dma = pltpu.SemaphoreType.DMA
    dq, dkv = pl.pallas_call(
        functools.partial(kernel, ctx_count),
        out_shape=(
            jax.ShapeDtypeStruct((LOCAL, TILE, DH), bf16),
            jax.ShapeDtypeStruct(tile, bf16),
        ),
        in_specs=[vmem] * 4,
        out_specs=(vmem, vmem),
        scratch_shapes=[
            pltpu.VMEM((WINDOW,) + tile, bf16),
            pltpu.VMEM((4, 4) + tile, bf16),
            pltpu.VMEM((4,) + tile, bf16),
            pltpu.VMEM((4,) + tile, bf16),
            pltpu.VMEM((3, 2) + halved, bf16),
            pltpu.VMEM((3, 2) + tile, bf16),
            pltpu.VMEM((2,) + tile, bf16),
            pltpu.VMEM(tile, f32),
            pltpu.VMEM((2,) + tile, f32),
            pltpu.VMEM((LOCAL, DH, TILE), f32),
            row, row, row,
            dma((3, 4)), dma((WINDOW,)), dma((2,)), dma((WINDOW,)), dma((WINDOW,)),
            dma((2, 4)), dma((4,)), dma((4,)), dma((3, 4)), dma((3, 4)), dma((2,)), dma((2,)),
        ],
        compiler_params=pltpu.CompilerParams(
            collective_id=0, has_side_effects=True, vmem_limit_bytes=56 << 20
        ),
        cost_estimate=pl.CostEstimate(
            flops=48 * 7 * 2 * TILE * TILE * DH,
            bytes_accessed=4 << 20,
            transcendentals=48 * 2 * TILE * TILE,
        ),
        name="attention_backward",
    )(
        firsts,
        queries.reshape(LOCAL, TILE, DH),
        grad_out.reshape(LOCAL, TILE, DH),
        kv_cache,
    )
    return dq.reshape(LOCAL * TILE, DH), dkv


def solution(mesh):
    placed = (P("ctx", "grp"), P(("ctx", "grp"), None), P("ctx", "grp"), P())
    return jax.shard_map(
        shards,
        mesh=mesh,
        in_specs=placed,
        out_specs=(P("ctx", "grp"), P(("ctx", "grp"), None)),
        check_vma=False,
    )
```

time: 688 us -> 104 us (0.15); the launches traced: 678 us -> 102 us
  waiting for transfers between devices: 497 us -> 0 us
  Pallas kernels: 0 us -> 97.2 us
  local copies, waits for them, and re-layouts: 61 us -> 4.03 us
  other arithmetic: 35.9 us -> 0.35 us
  loops' own time: 30.4 us -> 0 us
  matrix products: 26.5 us -> 0 us
  between operations: 14.1 us -> 0.66 us
  starting transfers between devices: 13.3 us -> 0 us
    ppermute x6 -> x0, waiting for transfers between devices: 271 us -> none  [passed_along(): return lax.ppermute(shard, axis, pairs)]
    reduce_scatter x1 -> x0, waiting for transfers between devices: 196 us -> none  [shards(): owned = lax.psum_scatter(own_block, 'grp', scatter_dimension=0, tiled=True)]
    pallas_call x0 -> x1, Pallas kernels: none -> 97.2 us  [shards(): pl.pallas_call(functools.partial(kernel, ctx_count), out_shape=(jax.Shape...]
    squeeze x34 -> x0, local copies, waits for them, and re-layouts: 32.9 us -> none  [the longest x30 29.2 us: scores_at(): lax.dynamic_index_in_dim(window, key_pos - window_base, 0, keepdims=False)]
    another operation x13 -> x0, loops' own time: 30.4 us -> none  [the longest x4 21.2 us: per_tile(): lax.fori_loop(first_tile, tile_pos + 1, third_pass, start_grad)]
    all_gather x1 -> x0, waiting for transfers between devices: 30.3 us -> none  [shards(): group_block = lax.all_gather(kv_cache, 'grp', axis=0, tiled=True)]
    dot_general x70 -> x0, matrix products: 26.5 us -> none  [the longest x20 7.73 us: scores_at(): jnp.einsum('qhd,kd->hqk', q_tile, kv_tile[:, :head_dim], preferred_elemen...]
    dynamic_update_slice x10 -> x0, other arithmetic: 19.3 us -> none  [third_pass(): lax.dynamic_update_index_in_dim(grad_window, updated, slot_pos, 0)]
  transfers between devices with their start and end apart: 8 -> 0, of which waited for: 6 -> 0; matrix products, arithmetic and copies ran while one was open for 1% -> 0% of each run, Pallas kernels for 0% -> 0%
where the time goes in v1:
time: 104 us; the launch traced here: 102 us
  Pallas kernels  97.2 us (93%)
  local copies, waits for them, and re-layouts  4.03 us (4%)
    pallas_call x1, Pallas kernels, shards(): pl.pallas_call(functools.partial(kernel, ctx_count), out_shape=(jax.Shape...  97.2 us
    unnamed x6, local copies, waits for them, and re-layouts  3.27 us

profile of v1, /device:TPU:16, one launch (start us, length us, event | category | flops | bytes accessed | tf_op | source)
XLA Modules:
  0.0 102.2 jit_solution(11544057161664605293)
XLA Ops:
  0.6 0.0 copy-start.1
  0.6 0.6 copy-done.1
  1.3 0.1 copy.8
  1.4 0.1 reduce-window.8
  1.4 0.1 reduce
  1.6 0.1 select_reduce_fusion
  1.7 0.1 dynamic-slice_subtract_fusion
  1.7 0.7 broadcast_in_dim.13.first_ref
  2.4 97.2 %attention_backward.1 = (bf16[4,512,128]{2,1,0:T(8,128)(2,1)}, bf16[512,256]{1,0:T(8,128)(2,1)}) custom-call(s32[4,1,512]{2,1,0:T(1,128)} %broadcast_in_dim.13.first_ref, bf16[4,512,128]{2,1,0:T(8,128)(2,1)} %bitcast.6, bf16[4,512,128]{2,1,0:T(8,128)(2,1)} %bitcast.7, bf16[512,256]{1,0:T(8,128)(2,1)} %kv_ref.1), custom_call_target="tpu_custom_call" | custom-call | flops 22548578304 | bytes 4194304 | tf_op jit(solution)/shard_map/attention_backward/pallas_call | solution.py:458
  99.6 0.0 copy-start
  99.6 1.9 %copy.11 = bf16[2048,128]{1,0:T(8,128)(2,1)} copy(bf16[2048,128]{1,0:T(8,128)(2,1)} %bitcast.4) | data formatting | bytes 1048576
  101.5 0.0 copy-done
  101.5 0.7 copy.12
  (1 shorter events, 0.0 us)
Async XLA Ops:
  0.6 0.7 copy-start.1
  99.6 1.9 %copy-start = (bf16[512,256]{1,0:T(8,128)(2,1)S(1)}, bf16[512,256]{1,0:T(8,128)(2,1)}, u32[]{:S(2)}) copy-start(bf16[512,256]{1,0:T(8,128)(2,1)} %get-tuple-element.9) | copy-start | bytes 786436

commit v2 on v1

v2 whole, which is shorter than its diff:
```python
import functools
import math

import jax
import jax.numpy as jnp
from jax import lax
from jax.experimental import pallas as pl
from jax.experimental.pallas import tpu as pltpu
from jax.sharding import PartitionSpec as P

DH = 128
TILE = 512
HALF = TILE // 2
LOCAL = 4
WINDOW = 16
SCALE = 1.0 / math.sqrt(DH)
C = SCALE * math.log2(math.e)
LOW = -1e30
f32 = jnp.float32
bf16 = jnp.bfloat16
MESH = pl.DeviceIdType.MESH


def dot(a, b, dims):
    return lax.dot_general(a, b, (dims, ((), ())), preferred_element_type=f32)


NT = ((1,), (1,))
NN = ((1,), (0,))


def kernel(
    ctx_count,
    doc_ref, q_hbm, g_hbm, kv_hbm,
    dq_hbm, dkv_hbm,
    q_ref, g_ref, dq_ref, dkv_ref, local_sem, kvw, stage, ddA, ddB, half, full, xin, acc, own, dqt, m_s, l_s, d_s, first_s,
    e_s, dp_s, top_s, p_all, ds_all,
    sendG, sendD, sendX, recvA, recvB,
    bsendD, brecvA, brecvB, bsendG, brecvG, bsendX, brecvX,
):
    c = lax.axis_index("ctx")
    y = lax.axis_index("grp")
    k = lax.rem(c, 2)
    other = c + 1 - 2 * k
    yR, yO, yL = (y + 1) % 4, (y + 2) % 4, (y + 3) % 4
    up = lambda n: (c + n) % ctx_count
    down = lambda n: (c + ctx_count - n) % ctx_count

    def remote(src, dst, ssem, rsem, dev):
        return pltpu.make_async_remote_copy(
            src_ref=src, dst_ref=dst, send_sem=ssem, recv_sem=rsem, device_id=dev, device_id_type=MESH
        )

    def landed(ref, sem):
        remote(ref, ref, sem, sem, (other, y)).wait_recv()

    def gone(ref, sem):
        remote(ref, ref, sem, sem, (other, y)).wait_send()

    barrier = pltpu.get_barrier_semaphore()
    far = (c + ctx_count + 6 * k - 3) % ctx_count
    for dev in ((other, y), (c, yR), (c, yL), (up(2), y), (down(2), y), (far, y)):
        pl.semaphore_signal(barrier, inc=1, device_id=dev, device_id_type=MESH)

    kv_in = pltpu.make_async_copy(kv_hbm, kvw.at[12 + y], local_sem.at[0])
    q_in = pltpu.make_async_copy(q_hbm, q_ref, local_sem.at[1])
    g_in = pltpu.make_async_copy(g_hbm, g_ref, local_sem.at[2])
    kv_in.start()
    q_in.start()
    g_in.start()

    begin = jnp.int32(0)
    firsts = [jnp.int32(0)] * LOCAL
    for doc in range(doc_ref.shape[0]):
        firsts = [
            jnp.where(begin <= c * LOCAL + t, begin, firsts[t]) for t in range(LOCAL)
        ]
        begin = begin + doc_ref[doc]
    for t in range(LOCAL):
        first_s[t] = jnp.full((1, TILE), firsts[t] - (c * LOCAL - 12), jnp.int32)
    m_s[...] = jnp.full_like(m_s, LOW)
    l_s[...] = jnp.zeros_like(l_s)
    d_s[...] = jnp.zeros_like(d_s)

    kv_in.wait()
    pl.semaphore_wait(barrier, 6)

    def share(group, base):
        src = kvw.at[base + y]
        remote(src, src, sendG.at[group, 0], recvA.at[base + y], (c, yR)).start()
        remote(src, src, sendG.at[group, 1], recvA.at[base + y], (c, yL)).start()

    def relay(group, base):
        landed(kvw.at[base + yL], recvA.at[base + yL])
        top = kvw.at[base + yL, pl.ds(0, HALF)]
        remote(top, top, sendG.at[group, 2], recvA.at[base + yL], (c, yR)).start()
        landed(kvw.at[base + yR], recvA.at[base + yR])
        low = kvw.at[base + yR, pl.ds(HALF, HALF)]
        remote(low, low, sendG.at[group, 3], recvB.at[base + yR], (c, yL)).start()

    def last_in(base):
        landed(kvw.at[base + yO, pl.ds(0, HALF)], recvA.at[base + yO])
        landed(kvw.at[base + yO, pl.ds(HALF, HALF)], recvB.at[base + yO])

    def across(src, dst):
        remote(kvw.at[src], kvw.at[dst], sendD.at[src], recvA.at[dst], (other, y)).start()

    def across_own(u):
        @pl.when(k == 0)
        def _():
            across(12 + u, 8 + u)

    def across_second(u):
        across(4 + u, 8 * k + u)

    share(0, 12)
    mine = kvw.at[12 + y]
    remote(mine, kvw.at[4 + y], sendX.at[0], recvA.at[4 + y], (up(2), y)).start()

    across_own(y)

    causal = lax.broadcasted_iota(jnp.int32, (TILE, TILE), 1) >= lax.broadcasted_iota(
        jnp.int32, (TILE, TILE), 0
    )

    def span(t, end=None):
        return slice(t * TILE, (t + 1 if end is None else end) * TILE)

    def forward_pair(slot, keys, values, t, diagonal, kept):
        scores = dot(keys, q_ref[span(t), :], NT) * C
        if diagonal:
            scores = jnp.where(causal, scores, LOW)
        m = m_s[t]
        valid = first_s[t] <= slot
        new_m = jnp.where(valid, jnp.maximum(m, jnp.max(scores, axis=0, keepdims=True)), m)
        e = jnp.exp2(scores - jnp.where(valid, new_m, -LOW))
        dp = dot(values, g_ref[span(t), :], NT)
        if kept:
            e_s[slot - 4, t] = e.astype(bf16)
            low = dp.astype(bf16)
            dp_s[slot - 4, t] = low
            top_s[slot - 4, t] = new_m
            dp = low.astype(f32)
        fade = jnp.exp2(m - new_m)
        m_s[t] = new_m
        l_s[t] = l_s[t] * fade + jnp.sum(e, axis=0, keepdims=True)
        d_s[t] = d_s[t] * fade + jnp.sum(e * dp, axis=0, keepdims=True)

    def split(slot):
        tile = kvw[slot]
        return tile[:, :DH], tile[:, DH:]

    def in_order(r):
        return (y + 3 * r - 5 * (r // 2) - 2 * (r // 3) + 4) % 4

    def each(u, body):
        for n in range(4):
            pl.when(u == n)(functools.partial(body, n))

    def forward_own(n):
        keys, values = split(12 + n)
        for t in range(n, LOCAL):
            forward_pair(12 + n, keys, values, t, t == n, False)

    def forward_far(n):
        if n:
            keys, values = split(n)
            for t in range(n):
                forward_pair(n, keys, values, t, False, False)

    def forward_step(j, carry):
        is_own = jnp.logical_or(j < 3, j == 5)

        @pl.when(j == 1)
        def _():
            @pl.when(k == 1)
            def _():
                gone(mine, sendX.at[0])
                remote(mine, kvw.at[y], sendX.at[1], recvA.at[y], (up(3), y)).start()

            relay(0, 12)
            across_own(yL)
            across_own(yR)
            landed(kvw.at[4 + y], recvA.at[4 + y])
            share(1, 4)
            across_second(y)

        @pl.when(j == 5)
        def _():
            last_in(12)
            remote(
                kvw.at[12 + yO], kvw.at[4 + yO], sendX.at[2], recvA.at[4 + yO], (up(2), y)
            ).start()
            across_own(yO)

            @pl.when(k == 0)
            def _():
                landed(kvw.at[y], recvA.at[y])
                share(2, 0)

        @pl.when(is_own)
        def _():
            each(in_order(j - 2 * (j // 5)), forward_own)

        @pl.when(jnp.logical_not(is_own))
        def _():
            i = j - 3 - j // 6
            r = i // 2
            u = in_order(r)
            base = 4 + 4 * ((i + k) % 2)

            @pl.when(i == 2)
            def _():
                landed(kvw.at[4 + yL], recvA.at[4 + yL])
                across_second(yL)
                landed(kvw.at[4 + yR], recvA.at[4 + yR])
                across_second(yR)

            @pl.when(i == 6)
            def _():
                landed(kvw.at[4 + yO], recvA.at[4 + yO])
                across_second(yO)

            @pl.when(jnp.logical_and(i == 5, k == 0))
            def _():
                relay(2, 0)

            @pl.when(base == 8)
            def _():
                landed(kvw.at[8 + u], recvA.at[8 + u])

            slot = base + u
            keys, values = split(slot)
            for t in range(LOCAL):
                forward_pair(slot, keys, values, t, False, True)

        return carry

    q_in.wait()
    g_in.wait()
    lax.fori_loop(0, 12, forward_step, 0)

    def forward_last(r, carry):
        u = in_order(r)

        @pl.when(k == 1)
        def _():
            landed(kvw.at[u], recvA.at[u])

        @pl.when(jnp.logical_and(k == 0, r == 3))
        def _():
            last_in(0)

        each(u, forward_far)
        return carry

    lax.fori_loop(0, 4, forward_last, 0)

    for t in range(LOCAL):
        total = l_s[t]
        m_s[t] = m_s[t] + jnp.log2(total)
        d_s[t] = d_s[t] / total
    dqt[...] = jnp.zeros_like(dqt)

    def settle(group, base):
        gone(kvw.at[base + y], sendG.at[group, 0])
        gone(kvw.at[base + y], sendG.at[group, 1])
        gone(kvw.at[base + yL, pl.ds(0, HALF)], sendG.at[group, 2])
        gone(kvw.at[base + yR, pl.ds(HALF, HALF)], sendG.at[group, 3])

    settle(0, 12)
    gone(kvw.at[4 + y], sendG.at[1, 0])
    gone(kvw.at[4 + y], sendG.at[1, 1])
    gone(kvw.at[12 + yO], sendX.at[2])
    for u in range(4):
        gone(kvw.at[4 + u], sendD.at[4 + u])

    @pl.when(k == 0)
    def _():
        settle(2, 0)
        gone(mine, sendX.at[0])
        for u in range(4):
            gone(kvw.at[12 + u], sendD.at[12 + u])

    @pl.when(k == 1)
    def _():
        gone(mine, sendX.at[1])

    def kept_pair(slot, t):
        p = e_s[slot - 4, t].astype(f32) * jnp.exp2(top_s[slot - 4, t] - m_s[t])
        ds_all[:, span(t)] = (p * (dp_s[slot - 4, t].astype(f32) - d_s[t])).astype(bf16)
        p_all[:, span(t)] = p.astype(bf16)

    def fresh_pair(slot, keys, values, t, diagonal):
        x = dot(keys, q_ref[span(t), :], NT) * C - jnp.where(first_s[t] <= slot, m_s[t], -LOW)
        if diagonal:
            x = jnp.where(causal, x, LOW)
        p = jnp.exp2(x)
        dp = dot(values, g_ref[span(t), :], NT)
        ds_all[:, span(t)] = (p * (dp - d_s[t])).astype(bf16)
        p_all[:, span(t)] = p.astype(bf16)

    def products(keys_t, begin, end):
        rows = span(begin, end)
        acc[:, :DH] = dot(ds_all[:, rows], q_ref[rows, :], NN)
        acc[:, DH:] = dot(p_all[:, rows], g_ref[rows, :], NN)
        dqt[:, rows] += dot(keys_t, ds_all[:, rows], NN)

    def turned(keys):
        return keys.astype(f32).T.astype(bf16)

    def backward_kept(slot):
        keys_t = turned(kvw[slot][:, :DH])
        for t in range(LOCAL):
            kept_pair(slot, t)
        products(keys_t, 0, LOCAL)

    def backward_far(n):
        if n == 0:
            acc[...] = jnp.zeros_like(acc)
        else:
            keys, values = split(n)
            for t in range(n):
                fresh_pair(n, keys, values, t, False)
            products(turned(keys), 0, n)

    def backward_own(n):
        keys, values = split(12 + n)
        for t in range(n, LOCAL):
            fresh_pair(12 + n, keys, values, t, t == n)
        products(turned(keys), n, LOCAL)

    def to_y(r):
        return (y + 2 - r + 3 * (r // 2) - 2 * (r // 3) + 4) % 4

    def send_halves(group):
        part = stage.at[group, yO]
        remote(
            part.at[pl.ds(0, HALF)], half.at[group, 0],
            bsendG.at[group, 0], brecvG.at[group, 0], (c, yR),
        ).start()
        remote(
            part.at[pl.ds(HALF, HALF)], half.at[group, 1],
            bsendG.at[group, 1], brecvG.at[group, 1], (c, yL),
        ).start()

    def send_right(group):
        part = stage.at[group, yR]
        remote(part, full.at[group, 0], bsendG.at[group, 2], brecvG.at[group, 2], (c, yR)).start()

    def send_left(group):
        part = stage.at[group, yL]
        remote(part, full.at[group, 1], bsendG.at[group, 3], brecvG.at[group, 3], (c, yL)).start()

    def reduce_step(group, r, keep):
        @pl.when(r == 0)
        def _():
            stage[group, yO] = acc[...].astype(bf16)
            send_halves(group)

        @pl.when(r == 1)
        def _():
            landed(half.at[group, 0], brecvG.at[group, 0])
            acc[:HALF] += half[group, 0].astype(f32)
            stage[group, yR] = acc[...].astype(bf16)
            send_right(group)

        @pl.when(r == 2)
        def _():
            landed(half.at[group, 1], brecvG.at[group, 1])
            acc[HALF:] += half[group, 1].astype(f32)
            stage[group, yL] = acc[...].astype(bf16)
            send_left(group)

        @pl.when(r == 3)
        def _():
            keep[...] = acc[...]

    def second_step(r):
        @pl.when(r == 0)
        def _():
            stage[1, yO] = acc[...].astype(bf16)
            remote(stage.at[1, yO], xin.at[2], bsendX.at[2], brecvX.at[2], (down(2), y)).start()

        @pl.when(r == 1)
        def _():
            stage[1, yR] = acc[...].astype(bf16)
            send_right(1)

        @pl.when(r == 2)
        def _():
            stage[1, yL] = acc[...].astype(bf16)
            send_left(1)

        @pl.when(r == 3)
        def _():
            own[1] = acc[...]

    def reduced(group, keep):
        landed(full.at[group, 0], brecvG.at[group, 2])
        landed(full.at[group, 1], brecvG.at[group, 3])
        return keep[...] + full[group, 0].astype(f32) + full[group, 1].astype(f32)

    def reduce_gone(group):
        if group == 1:
            gone(stage.at[1, yO], bsendX.at[2])
        else:
            gone(stage.at[group, yO, pl.ds(0, HALF)], bsendG.at[group, 0])
            gone(stage.at[group, yO, pl.ds(HALF, HALF)], bsendG.at[group, 1])
        gone(stage.at[group, yR], bsendG.at[group, 2])
        gone(stage.at[group, yL], bsendG.at[group, 3])

    def backward_first(r, carry):
        u = to_y(r)
        each(u, backward_far)

        @pl.when(jnp.logical_and(k == 0, r < 3))
        def _():
            stage[2, u] = acc[...].astype(bf16)

            @pl.when(r == 0)
            def _():
                send_halves(2)

        @pl.when(jnp.logical_and(k == 0, r == 3))
        def _():
            own[1] = acc[...]

        @pl.when(k == 1)
        def _():
            stage[2, u] = acc[...].astype(bf16)
            remote(stage.at[2, u], ddA.at[u], bsendD.at[0, u], brecvA.at[u], (other, y)).start()

        return carry

    lax.fori_loop(0, 4, backward_first, 0)

    def early(r):
        u = to_y(r)
        backward_kept(8 + u)
        stage[3, u] = acc[...].astype(bf16)
        remote(stage.at[3, u], ddB.at[u], bsendD.at[1, u], brecvB.at[u], (other, y)).start()

        @pl.when(jnp.logical_and(r == 0, k == 0))
        def _():
            landed(half.at[2, 0], brecvG.at[2, 0])
            stage[2, yR, :HALF] += half[2, 0]
            send_right(2)
            landed(half.at[2, 1], brecvG.at[2, 1])
            stage[2, yL, HALF:] += half[2, 1]
            send_left(2)

        @pl.when(jnp.logical_and(r == 2, k == 0))
        def _():
            stage[2, y] = reduced(2, own.at[1]).astype(bf16)
            remote(stage.at[2, y], xin.at[1], bsendX.at[1], brecvX.at[1], (down(3), y)).start()

        backward_kept(4 + u)

        @pl.when(k == 0)
        def _():
            landed(ddA.at[u], brecvA.at[u])
            acc[...] += ddA[u].astype(f32)

        @pl.when(k == 1)
        def _():
            landed(ddB.at[u], brecvB.at[u])
            acc[...] += ddB[u].astype(f32)

        second_step(r)

    def late(r):
        u = to_y(r)
        each(u, backward_own)

        @pl.when(k == 0)
        def _():
            landed(ddB.at[u], brecvB.at[u])
            acc[...] += ddB[u].astype(f32)

        @pl.when(r == 0)
        def _():
            landed(xin.at[2], brecvX.at[2])
            acc[...] += xin[2].astype(f32)

        reduce_step(0, r, own.at[0])

        @pl.when(r == 1)
        def _():
            stage[1, y] = reduced(1, own.at[1]).astype(bf16)
            remote(stage.at[1, y], xin.at[0], bsendX.at[0], brecvX.at[0], (down(2), y)).start()

    def backward_step(r, carry):
        pl.when(r < 4)(functools.partial(early, r))
        pl.when(r >= 2)(functools.partial(late, r - 2))
        return carry

    lax.fori_loop(0, 6, backward_step, 0)

    for t in range(LOCAL):
        dq_ref[span(t), :] = (dqt[:, span(t)].T * SCALE).astype(bf16)
    dq_out = pltpu.make_async_copy(dq_ref, dq_hbm, local_sem.at[1])
    dq_out.start()

    landed(xin.at[0], brecvX.at[0])
    own[0] = own[0] + xin[0].astype(f32)

    @pl.when(k == 1)
    def _():
        landed(xin.at[1], brecvX.at[1])
        own[0] = own[0] + xin[1].astype(f32)

    total = reduced(0, own.at[0])
    dkv_ref[:, :DH] = (total[:, :DH] * SCALE).astype(bf16)
    dkv_ref[:, DH:] = total[:, DH:].astype(bf16)
    dkv_out = pltpu.make_async_copy(dkv_ref, dkv_hbm, local_sem.at[0])
    dkv_out.start()

    reduce_gone(0)
    reduce_gone(1)
    gone(stage.at[1, y], bsendX.at[0])
    for u in range(4):
        gone(stage.at[3, u], bsendD.at[1, u])

    @pl.when(k == 0)
    def _():
        reduce_gone(2)
        gone(stage.at[2, y], bsendX.at[1])

    @pl.when(k == 1)
    def _():
        for u in range(4):
            gone(stage.at[2, u], bsendD.at[0, u])
    dq_out.wait()
    dkv_out.wait()


def hand_over(dq_in, dkv_in, dq_out, dkv_out, dq_mid, dkv_mid, sem):
    legs = []
    for source, middle, target, parts in ((dq_in, dq_mid, dq_out, 4), (dkv_in, dkv_mid, dkv_out, 2)):
        rows = source.shape[0] // parts
        for n in range(parts):
            block = pl.ds(n * rows, rows)
            number = len(legs)
            legs.append((
                pltpu.make_async_copy(source.at[block], middle.at[block], sem.at[0, number]),
                pltpu.make_async_copy(middle.at[block], target.at[block], sem.at[1, number]),
            ))
    for fetch, _ in legs:
        fetch.start()
    for fetch, put in legs:
        fetch.wait()
        put.start()
    for _, put in legs:
        put.wait()


def shards(queries, kv_cache, grad_out, doc_tiles):
    ctx_count = lax.axis_size("ctx")
    anywhere = pl.BlockSpec(memory_space=pl.ANY)
    rows = pltpu.VMEM((LOCAL * TILE, DH), bf16)
    tile = (TILE, 2 * DH)
    halved = (HALF, 2 * DH)
    row = pltpu.VMEM((LOCAL, 1, TILE), f32)
    dma = pltpu.SemaphoreType.DMA
    dq, dkv = pl.pallas_call(
        functools.partial(kernel, ctx_count),
        out_shape=(
            jax.ShapeDtypeStruct((LOCAL * TILE, DH), bf16),
            jax.ShapeDtypeStruct(tile, bf16),
        ),
        in_specs=[pl.BlockSpec(memory_space=pltpu.SMEM)] + [anywhere] * 3,
        out_specs=(anywhere, anywhere),
        scratch_shapes=[
            rows, rows, rows,
            pltpu.VMEM(tile, bf16),
            pltpu.SemaphoreType.DMA((3,)),
            pltpu.VMEM((WINDOW,) + tile, bf16),
            pltpu.VMEM((4, 4) + tile, bf16),
            pltpu.VMEM((4,) + tile, bf16),
            pltpu.VMEM((4,) + tile, bf16),
            pltpu.VMEM((3, 2) + halved, bf16),
            pltpu.VMEM((3, 2) + tile, bf16),
            pltpu.VMEM((3,) + tile, bf16),
            pltpu.VMEM(tile, f32),
            pltpu.VMEM((2,) + tile, f32),
            pltpu.VMEM((DH, LOCAL * TILE), f32),
            row, row, row,
            pltpu.VMEM((LOCAL, 1, TILE), jnp.int32),
            pltpu.VMEM((8, LOCAL, TILE, TILE), bf16),
            pltpu.VMEM((8, LOCAL, TILE, TILE), bf16),
            pltpu.VMEM((8, LOCAL, 1, TILE), f32),
            pltpu.VMEM((TILE, LOCAL * TILE), bf16),
            pltpu.VMEM((TILE, LOCAL * TILE), bf16),
            dma((3, 4)), dma((WINDOW,)), dma((3,)), dma((WINDOW,)), dma((WINDOW,)),
            dma((2, 4)), dma((4,)), dma((4,)), dma((3, 4)), dma((3, 4)), dma((3,)), dma((3,)),
        ],
        compiler_params=pltpu.CompilerParams(
            collective_id=0, has_side_effects=True, vmem_limit_bytes=60 << 20
        ),
        cost_estimate=pl.CostEstimate(
            flops=48 * 7 * 2 * TILE * TILE * DH,
            bytes_accessed=4 << 20,
            transcendentals=48 * 2 * TILE * TILE,
        ),
        name="attention_backward",
    )(
        doc_tiles, queries, grad_out, kv_cache,
    )
    return pl.pallas_call(
        hand_over,
        out_shape=(
            jax.ShapeDtypeStruct(dq.shape, bf16),
            jax.ShapeDtypeStruct(dkv.shape, bf16),
        ),
        in_specs=[anywhere] * 2,
        out_specs=(anywhere, anywhere),
        scratch_shapes=[rows, pltpu.VMEM(tile, bf16), dma((2, 6))],
        name="hand_over",
    )(dq, dkv)


def solution(mesh):
    placed = (P("ctx", "grp"), P(("ctx", "grp"), None), P("ctx", "grp"), P())
    return jax.shard_map(
        shards,
        mesh=mesh,
        in_specs=placed,
        out_specs=(P("ctx", "grp"), P(("ctx", "grp"), None)),
        check_vma=False,
    )
```

time: 104 us -> 80.1 us (0.77); the launches traced: 102 us -> 80 us
  Pallas kernels: 97.2 us -> 79.2 us
  local copies, waits for them, and re-layouts: 4.03 us -> 0 us
    pallas_call x1, Pallas kernels: 97.2 us -> 77.2 us  [shards(): pl.pallas_call(functools.partial(kernel, ctx_count), out_shape=(jax.Shape...]
    unnamed x6 -> x0, local copies, waits for them, and re-layouts: 3.27 us -> none
    pallas_call x0 -> x1, Pallas kernels: none -> 1.97 us  [shards(): pl.pallas_call(hand_over, out_shape=(jax.ShapeDtypeStruct(dq.shape, bf16)...]
where the time goes in v2:
time: 80.1 us; the launch traced here: 80 us
  Pallas kernels  79.2 us (99%)
    pallas_call x1, Pallas kernels, shards(): pl.pallas_call(functools.partial(kernel, ctx_count), out_shape=(jax.Shape...  77.2 us
    pallas_call x1, Pallas kernels, shards(): pl.pallas_call(hand_over, out_shape=(jax.ShapeDtypeStruct(dq.shape, bf16)...  1.97 us

profile of v2, /device:TPU:16, one launch (start us, length us, event | category | flops | bytes accessed | tf_op | source)
XLA Modules:
  0.0 80.0 jit_solution(8798080977872434959)
XLA Ops:
  0.6 77.2 %attention_backward.1 = (bf16[2048,128]{1,0:T(8,128)(2,1)}, bf16[512,256]{1,0:T(8,128)(2,1)}) custom-call(s32[32]{0:T(128)} %doc_ref.1, bf16[2048,128]{1,0:T(8,128)(2,1)} %q_hbm.1, bf16[2048,128]{1,0:T(8,128)(2,1)} %g_hbm.1, bf16[512,256]{1,0:T(8,128)(2,1)} %kv_hbm.1), custom_call_target="tpu_custom_call" | custom-call | flops 22548578304 | bytes 4194304 | tf_op jit(solution)/shard_map/attention_backward/pallas_call | solution.py:566
  77.9 2.0 %hand_over.1 = (bf16[2048,128]{1,0:T(8,128)(2,1)}, bf16[512,256]{1,0:T(8,128)(2,1)}) custom-call(bf16[2048,128]{1,0:T(8,128)(2,1)} %get-tuple-element.4.dq_in, bf16[512,256]{1,0:T(8,128)(2,1)} %get-tuple-element.5.dkv_in), custom_call_target="tpu_custom_call" | custom-call | tf_op jit(solution)/shard_map/hand_over/pallas_call | solution.py:610
